TPU v7x, 32 devices: a whole 2x2x4 slice. The times are simulated.
32 devices in a mesh: req: 8 (over y, x, core), tp: 4 (over z).
Axes of the slice: x: 2, y: 2, z: 4, core: 2. Of those that a mesh axis runs over, the one named last changes fastest.
Arguments:
- activations: bfloat16 [2048, 2304], P('req'), may hold values from -6 to 6
- lengths: int32 [8, 4], P('req'), may hold values from 1 to 192, 256 in all within a row
- adapter_of: int32 [8, 4], P('req'), may hold values from 0 to 15
- slot_of: int32 [16], replicated, may hold values from 0 to 15, as said below
- page_table: int32 [8, 6], P('req'), may hold values from 0 to 5, each once within a row
- experts_of: int32 [2048, 2], P('req'), may hold values from 0 to 7, all different within a row; in each aligned block of 256 rows (0 to 255, 256 to 511, ...) at most 72 rows name the same one
- attn_gain: float32 [2304], replicated, may hold values from 0.25 to 1.75
- moe_gain: float32 [2304], replicated, may hold values from 0.25 to 1.75
- w_qkv: bfloat16 [2304, 3, 2304], P(None, None, 'tp'), may hold values from -4 to 4
- output_weight: bfloat16 [2304, 2304], P('tp'), may hold values from -0.125 to 0.125
- router: bfloat16 [2304, 8], replicated, may hold values from -0.125 to 0.125
- w_gate_up: bfloat16 [8, 2304, 2, 5760], P('req', None, None, 'tp'), may hold values from -0.125 to 0.125
- w_down: bfloat16 [8, 5760, 2304], P('req', 'tp'), may hold values from -0.078125 to 0.078125
- expert_up_factors: bfloat16 [8, 256, 2, 5760], P('req', None, None, 'tp'), may hold values from -0.59765625 to 0.59765625
- pool_a: bfloat16 [16, 2304, 64], P('req'), may hold values from -0.125 to 0.125
- slot_query_key_value_up: bfloat16 [16, 16, 3, 2304], P('req', None, None, 'tp'), may hold values from -0.59765625 to 0.59765625
- pool_aout: bfloat16 [16, 2304, 16], P('req', 'tp'), may hold values from -0.125 to 0.125
- pool_bout: bfloat16 [16, 16, 2304], P('req'), may hold values from -1.796875 to 1.796875
Outputs:
- layer_out: bfloat16 [2048, 2304], P('req')
- page_cache: bfloat16 [48, 128, 2, 2304], P('req', None, None, 'tp')
Inputs may be any that keep to these rules, and one draw needn't show every extreme that they name: `slot_of`: distinct slots. `page_table`: each row holds every page index once. `experts_of`: the two experts of a token differ; among the 256 tokens of one index of req at most 72 choose one expert, and some expert reaches 72.
All inputs are finite; a program needn't handle non-finite values.
Results may differ from a plain program's by a relative error of at most 0.0095.
Values may be sent and summed in bfloat16 or wider, within the bound.
A program may use at most 128 MiB of HBM per device.

v0:
```python
import math
import jax
import jax.numpy as jnp
from jax import lax
from jax.sharding import PartitionSpec as P

D = 2304
HEAD_SIZE = 64
EXPERTS = 8
ADAPTER_RANK = 16
ADAPTER_TOTAL = 16
PAGE = 128
CAP = 72
epsilon = 1e-05
adapter_scale = 2.0
rope_base = 10000.0


def rms_norm(values, scales):
    mean_sq = jnp.mean(values * values, axis=-1, keepdims=True)
    return values * lax.rsqrt(mean_sq + epsilon) * scales


def token_layout(lengths_row, tok_count):
    ends_at = jnp.cumsum(lengths_row)
    starts = ends_at - lengths_row
    places = jnp.arange(tok_count, dtype=jnp.int32)
    request = jnp.sum((places[:, None] >= ends_at[None, :]).astype(jnp.int32), axis=1)
    position = places - starts[request]
    return (request, position)


def rotate(values, position):
    head_dim = values.shape[-1]
    half_dim = head_dim // 2
    frequency = rope_base ** (-jnp.arange(half_dim, dtype=jnp.float32) * 2.0 / head_dim)
    angles = position.astype(jnp.float32)[:, None] * frequency[None, :]
    cosine = jnp.cos(angles)[:, None, :]
    sine_part = jnp.sin(angles)[:, None, :]
    front_half = values[..., :half_dim]
    back_half = values[..., half_dim:]
    return jnp.concatenate(
        [front_half * cosine - back_half * sine_part, back_half * cosine + front_half * sine_part],
        axis=-1,
    )


def per_device(
    activations,
    lengths,
    adapter_of,
    slot_of,
    page_table,
    experts_of,
    attn_gain,
    moe_gain,
    w_qkv,
    output_weight,
    router,
    w_gate_up,
    w_down,
    expert_up_factors,
    pool_a,
    slot_query_key_value_up,
    pool_aout,
    pool_bout,
):
    token_share = activations.shape[0]
    n_req = lax.axis_size("req")
    request, position = token_layout(lengths[0], token_share)
    adapter = adapter_of[0][request]
    token_slot = slot_of[adapter]
    pool_down, slot_up_factors, pool_head, pool_outup = (
        lax.all_gather(pool_a, "req", axis=0, tiled=True),
        lax.all_gather(slot_query_key_value_up, "req", axis=0, tiled=True),
        lax.all_gather(pool_aout, "req", axis=0, tiled=True),
        lax.all_gather(pool_bout, "req", axis=0, tiled=True),
    )
    slot_count = pool_down.shape[0]
    slot_hot = token_slot[:, None] == jnp.arange(slot_count, dtype=jnp.int32)[None, :]
    head_width = w_qkv.shape[2]
    heads_number = head_width // HEAD_SIZE
    normed = rms_norm(activations.astype(jnp.float32), attn_gain).astype(jnp.bfloat16)
    down_all = jnp.einsum(
        "td,sdr->tsr",
        normed,
        pool_down[:, :, : 3 * ADAPTER_RANK],
        preferred_element_type=jnp.float32,
    )
    coeff_qkv = jnp.sum(jnp.where(slot_hot[:, :, None], down_all, 0.0), axis=1).astype(jnp.bfloat16)
    spread_rows = jnp.where(
        slot_hot[:, :, None, None],
        coeff_qkv.reshape(token_share, 1, 3, ADAPTER_RANK),
        jnp.zeros((), jnp.bfloat16),
    )
    adapter_query_key_value = jnp.einsum(
        "qwxv,wvxd->qxd", spread_rows, slot_up_factors, preferred_element_type=jnp.float32
    )
    plain_query_key_value = jnp.dot(
        normed, w_qkv.reshape(D, 3 * head_width), preferred_element_type=jnp.float32
    ).reshape(token_share, 3, head_width)
    projection_result = (plain_query_key_value + adapter_scale * adapter_query_key_value).reshape(
        token_share, 3, heads_number, HEAD_SIZE
    )
    queries = rotate(projection_result[:, 0], position).astype(jnp.bfloat16)
    keys_roped = rotate(projection_result[:, 1], position).astype(jnp.bfloat16)
    values = projection_result[:, 2].astype(jnp.bfloat16)
    pool_dev = page_table.shape[1]
    pages_used = (lengths[0] + PAGE - 1) // PAGE
    first_page = jnp.cumsum(pages_used) - pages_used
    local_page = page_table[0][first_page[request] + position // PAGE]
    cache_row = local_page * PAGE + position % PAGE
    place_hot = (
        jnp.arange(pool_dev * PAGE, dtype=jnp.int32)[:, None] == cache_row[None, :]
    ).astype(jnp.bfloat16)
    key_value = jnp.stack(
        [keys_roped.reshape(token_share, head_width), values.reshape(token_share, head_width)],
        axis=1,
    ).reshape(token_share, 2 * head_width)
    page_cache = (
        jnp.dot(place_hot, key_value, preferred_element_type=jnp.float32)
        .astype(jnp.bfloat16)
        .reshape(pool_dev, PAGE, 2, head_width)
    )
    scores = jnp.einsum("qhd,khd->hqk", queries, keys_roped, preferred_element_type=jnp.float32) * (
        1.0 / math.sqrt(HEAD_SIZE)
    )
    allowed = (request[:, None] == request[None, :]) & (position[None, :] <= position[:, None])
    scores = jnp.where(allowed[None], scores, -1e30)
    row_max = jnp.max(scores, axis=-1, keepdims=True)
    weights = jnp.exp(scores - row_max)
    weights = (weights / jnp.sum(weights, axis=-1, keepdims=True)).astype(jnp.bfloat16)
    attention_result = (
        jnp.einsum("hqk,khd->qhd", weights, values, preferred_element_type=jnp.float32)
        .astype(jnp.bfloat16)
        .reshape(token_share, head_width)
    )
    aout_all = jnp.einsum(
        "tc,scr->tsr", attention_result, pool_head, preferred_element_type=jnp.float32
    )
    coeff_out = jnp.sum(jnp.where(slot_hot[:, :, None], aout_all, 0.0), axis=1)
    spread_out = jnp.where(slot_hot[:, :, None], coeff_out[:, None, :], 0.0).reshape(
        token_share, slot_count * ADAPTER_RANK
    )
    output_update = jnp.dot(
        spread_out,
        pool_outup.astype(jnp.float32).reshape(slot_count * ADAPTER_RANK, D),
        precision=lax.Precision.HIGHEST,
    )
    head_term = (
        jnp.dot(attention_result, output_weight, preferred_element_type=jnp.float32)
        + adapter_scale * output_update
    )
    mixed_out = lax.psum(head_term, "tp")
    residual_stream = activations.astype(jnp.float32) + mixed_out
    normed_moe = rms_norm(residual_stream, moe_gain).astype(jnp.bfloat16)
    logits = jnp.dot(normed_moe, router, preferred_element_type=jnp.float32)
    chosen = jnp.take_along_axis(logits, experts_of, axis=1)
    gate_weights = 1.0 / (1.0 + jnp.exp(chosen[:, ::-1] - chosen))
    exp_all = jnp.einsum(
        "td,sdr->tsr",
        normed_moe,
        pool_down[:, :, 3 * ADAPTER_RANK :],
        preferred_element_type=jnp.float32,
    )
    coeff_exp = jnp.sum(jnp.where(slot_hot[:, :, None], exp_all, 0.0), axis=1).astype(jnp.bfloat16)
    capacity = CAP
    split_count = n_req // EXPERTS
    flat_expert = experts_of.reshape(-1)
    expert_hot = (flat_expert[:, None] == jnp.arange(EXPERTS, dtype=jnp.int32)[None, :]).astype(
        jnp.int32
    )
    order_in = jnp.sum((jnp.cumsum(expert_hot, axis=0) - expert_hot) * expert_hot, axis=1)
    column = flat_expert * capacity + order_in
    pick = (column[:, None] == jnp.arange(EXPERTS * capacity, dtype=jnp.int32)[None, :]).reshape(
        token_share, 2, EXPERTS * capacity
    )
    route = jnp.any(pick, axis=1).astype(jnp.bfloat16)
    combine_weights = jnp.sum(jnp.where(pick, gate_weights[:, :, None], 0.0), axis=1)

    def spread_copies(array):
        shaped = array.reshape((EXPERTS, 1, capacity) + array.shape[1:])
        return jnp.broadcast_to(shaped, (EXPERTS, split_count, capacity) + array.shape[1:]).reshape(
            (n_req, capacity) + array.shape[1:]
        )

    send_coeff = jnp.einsum(
        "ts,tr->sr", route, coeff_exp, preferred_element_type=jnp.float32
    ).astype(jnp.bfloat16)
    send_ids = jnp.einsum(
        "ts,t->s", route, adapter.astype(jnp.bfloat16), preferred_element_type=jnp.float32
    ).astype(jnp.bfloat16)
    adapter_range = jnp.arange(ADAPTER_TOTAL, dtype=jnp.int32).astype(jnp.bfloat16)
    send_rows = jnp.einsum(
        "ts,td->sd", route, normed_moe, preferred_element_type=jnp.float32
    ).astype(jnp.bfloat16)
    expert_input_rows = lax.all_to_all(
        spread_copies(send_rows), "req", split_axis=0, concat_axis=0, tiled=True
    )
    coeff_rank = lax.all_to_all(
        spread_copies(send_coeff), "req", split_axis=0, concat_axis=0, tiled=True
    )
    adapter_ids = lax.all_to_all(
        spread_copies(send_ids), "req", split_axis=0, concat_axis=0, tiled=True
    )
    count = expert_input_rows.shape[1]
    flat_rows = expert_input_rows.reshape(n_req * count, D)
    flat_coeff = coeff_rank.reshape(n_req * count, ADAPTER_RANK)
    flat_ids = adapter_ids.reshape(n_req * count)
    unit_count = w_gate_up.shape[3]
    broad_coefficients = jnp.where(
        flat_ids[:, None, None] == adapter_range[None, :, None],
        flat_coeff[:, None, :],
        jnp.zeros((), jnp.bfloat16),
    ).reshape(n_req * count, ADAPTER_TOTAL * ADAPTER_RANK)
    before_norm = jnp.dot(
        flat_rows, w_gate_up[0].reshape(D, 2 * unit_count), preferred_element_type=jnp.float32
    )
    before_norm = before_norm + adapter_scale * jnp.dot(
        broad_coefficients,
        expert_up_factors[0].reshape(ADAPTER_TOTAL * ADAPTER_RANK, 2 * unit_count),
        preferred_element_type=jnp.float32,
    )
    hidden = (jax.nn.silu(before_norm[:, :unit_count]) * before_norm[:, unit_count:]).astype(
        jnp.bfloat16
    )
    partial_term = jnp.dot(hidden, w_down[0], preferred_element_type=jnp.float32).astype(
        jnp.bfloat16
    )
    returned = lax.all_to_all(
        partial_term.reshape(n_req, count, D), "req", split_axis=0, concat_axis=0, tiled=True
    )
    summed = jnp.sum(
        returned.astype(jnp.float32).reshape(EXPERTS, split_count, capacity, D), axis=1
    ).reshape(EXPERTS * capacity, D)
    moe_part = jnp.dot(combine_weights, summed, precision=lax.Precision.HIGHEST)
    moe_sum = lax.psum(moe_part.astype(jnp.bfloat16), "tp").astype(jnp.float32)
    layer_out = (residual_stream + moe_sum).astype(jnp.bfloat16)
    return (layer_out, page_cache)


def solution(mesh):
    return jax.shard_map(
        per_device,
        mesh=mesh,
        in_specs=(
            P("req", None),
            P("req", None),
            P("req", None),
            P(),
            P("req", None),
            P("req", None),
            P(),
            P(),
            P(None, None, "tp"),
            P("tp", None),
            P(),
            P("req", None, None, "tp"),
            P("req", "tp", None),
            P("req", None, None, "tp"),
            P("req", None, None),
            P("req", None, None, "tp"),
            P("req", "tp", None),
            P("req", None, None),
        ),
        out_specs=(P("req", None), P("req", None, None, "tp")),
        check_vma=False,
    )
```

profile of v0, /device:TPU:0, one launch (start us, length us, event | category | flops | bytes accessed | tf_op | source)
XLA Modules:
  0.0 364.0 jit_solution(4491412793175182737)
XLA Ops:
  11.3 1.6 fusion.10
  12.9 1.5 fusion.63
  14.3 1.5 fusion.66
  15.8 2.0 fusion.62
  17.8 6.8 %compare_select_fusion.9 = (s32[256,1]{0,1:T(1,128)S(1)}, s32[256,1]{0,1:T(1,128)S(1)}, s32[256,1]{0,1:T(1,128)S(1)}) fusion(s32[]{:T(128)} %bitcast.20, s32[]{:T(128)} %bitcast.21, s32[]{:T(128)} %bitcast.22, s32[]{:T(128)} %bitcast.23, s32[]{:T(128)} %bitcast.24, s32[]{:T(128)} %bitcast.26, s32[]{:T(128)} %bitcast.25, s32[]{:T(128)} %bitcast.10, ...), kind=kLoop, calls=%fused_computation.105 | loop fusion | flops 6144 | bytes 4140 | tf_op jit(solution)/shard_map/gather | solution.py:72
  24.6 5.7 %select_select_fusion.2 = s32[256]{0:T(256)S(1)} fusion(pred[256]{0:T(512)(128)(4,1)S(1)} %get-tuple-element.22, pred[256]{0:T(512)(128)(4,1)S(1)} %get-tuple-element.21, pred[256]{0:T(512)(128)(4,1)S(1)} %get-tuple-element.20, pred[256]{0:T(512)(128)(4,1)S(1)} %get-tuple-element.19, pred[256]{0:T(512)(128)(4,1)S(1)} %get-tuple-element.18, ...), kind=kLoop, calls=%fused_computation.137 | loop fusion | flops 2304 | bytes 4388 | tf_op jit(solution)/shard_map/gather | solution.py:72
  31.0 8.8 %fusion.49 = (s32[256,1]{0,1:T(1,128)S(1)}, s32[256,1]{0,1:T(1,128)S(1)}) fusion(s32[]{:T(128)} %bitcast.71, s32[]{:T(128)} %bitcast.72, s32[]{:T(128)} %bitcast.73, s32[]{:T(128)} %bitcast.67, s32[]{:T(128)} %bitcast.74, s32[]{:T(128)} %bitcast.68, s32[]{:T(128)} %bitcast.76, s32[]{:T(128)} %bitcast.75, s32[]{:T(128)} %bitcast.70, s32[]{:T(128)} %bitcast.69, ...), kind=kLoop, calls=%fused_computation.132 | loop fusion | flops 11008 | bytes 3128 | tf_op jit(solution)/shard_map/mul | solution.py:112
  40.0 12.0 %all_gather.14 = bf16[16,576,16]{1,2,0:T(8,128)(2,1)S(1)} all-gather(bf16[2,576,16]{1,2,0:T(8,128)(2,1)} %param.34), channel_id=1, replica_groups=mesh['req'=8,'tp'=4] {'req'}, dimensions={0}, use_global_device_ids=true | all-gather | bytes 331776 | tf_op jit(solution)/shard_map/all_gather | solution.py:76
  52.0 12.0 %all_gather.13 = bf16[16,16,3,576]{3,1,2,0:T(8,128)(2,1)} all-gather(bf16[2,16,3,576]{3,1,2,0:T(8,128)(2,1)S(1)} %copy-done.14), channel_id=1, replica_groups=mesh['req'=8,'tp'=4] {'req'}, dimensions={0}, use_global_device_ids=true | all-gather | bytes 995328 | tf_op jit(solution)/shard_map/all_gather | solution.py:75
  64.2 6.8 %fusion.1 = f32[256,3,576]{0,2,1:T(8,128)} fusion(bf16[2304,3,576]{0,2,1:T(8,128)(2,1)} %param.26, bf16[256,2304]{1,0:T(8,128)(2,1)S(1)} %copy-done.5, f32[2304]{0:T(1024)S(1)} %copy-done.18, f32[256]{0:T(256)S(1)} %add_rsqrt_fusion.1), kind=kOutput, calls=%fused_computation.2 | convolution fusion | flops 2040791040 | bytes 10921984 | tf_op jit(solution)/shard_map/dot_general | solution.py:99
  71.0 1.5 copy-done.6
  78.1 3.4 fusion.67
  81.5 2.2 convolution_convert_fusion.3
  84.1 2.5 fusion.8
  86.5 2.6 convolution_add_fusion
  93.1 3.4 all-to-all-start.1
  96.6 88.4 %all-reduce.3.cloned.1.call-done = f32[256,2304]{1,0:T(8,128)} async-done(((f32[256,2304]{1,0:T(8,128)}), f32[256,2304]{1,0:T(8,128)}) %all-reduce.3.cloned.1.call-update) | async-done | bytes 2359312 | tf_op jit(solution)/shard_map/psum | solution.py:154
  185.0 2.5 multiply_reduce_fusion
  190.9 3.7 %all-to-all-start.2 = ((bf16[8,72,16]{1,2,0:T(8,128)(2,1)}), bf16[8,72,16]{1,2,0:T(8,128)(2,1)S(1)}, u32[]{:S(2)}, u32[]{:S(2)}) async-start(bf16[8,72,16]{1,2,0:T(8,128)(2,1)} %copy.92), calls=%async_computation.2 | async-start | bytes 65536 | tf_op jit(solution)/shard_map/all_to_all | solution.py:200
  194.6 3.7 %convolution_convert_fusion = bf16[576,2304]{1,0:T(8,128)(2,1)} fusion(pred[256,576]{0,1:T(8,128)(4,1)S(1)} %fusion.17, bf16[256,2304]{1,0:T(8,128)(2,1)} %copy-done.3), kind=kOutput, calls=%fused_computation.8 | convolution fusion | flops 680804352 | bytes 3981312 | tf_op jit(solution)/shard_map/ts,td->sd/dot_general | solution.py:194
  199.4 3.6 all-to-all-start
  203.5 32.1 %all-to-all-done = bf16[8,72,2304]{2,1,0:T(8,128)(2,1)S(1)} async-done(((bf16[8,72,2304]{2,1,0:T(8,128)(2,1)}), bf16[8,72,2304]{2,1,0:T(8,128)(2,1)S(1)}, u32[]{:S(2)}, u32[]{:S(2)}) %all-to-all-start) | async-done | bytes 2654240 | tf_op jit(solution)/shard_map/all_to_all | solution.py:197
  235.6 11.4 %fusion.72 = f32[576,2880]{1,0:T(8,128)S(1)} fusion(bf16[576,2304]{1,0:T(8,128)(2,1)S(1)} %bitcast.153, bf16[2304,2880]{0,1:T(8,128)(2,1)} %bitcast.173), kind=kOutput, calls=%fused_computation.165 | convolution fusion | flops 7644119040 | bytes 22560768 | tf_op jit(solution)/shard_map/dot_general | solution.py:216
  248.3 9.2 %fusion.5 = bf16[576,2304]{1,0:T(8,128)(2,1)} fusion(bf16[1,1440,2304]{2,1,0:T(8,128)(2,1)} %param.30, f32[576,2880]{1,0:T(8,128)S(1)} %multiply_add_fusion), kind=kOutput, calls=%fused_computation.7 | convolution fusion | flops 3828363264 | bytes 16367616 | tf_op jit(solution)/shard_map/dot_general | solution.py:227
  257.5 4.5 %all-to-all-start.3 = ((bf16[8,72,2304]{2,1,0:T(8,128)(2,1)}), bf16[8,72,2304]{2,1,0:T(8,128)(2,1)}, u32[]{:S(2)}, u32[]{:S(2)}) async-start(bf16[8,72,2304]{2,1,0:T(8,128)(2,1)} %bitcast.152), calls=%async_computation.3 | async-start | bytes 5308416 | tf_op jit(solution)/shard_map/all_to_all | solution.py:230
  263.0 3.6 gather_fusion
  267.1 27.5 %all-to-all-done.3 = bf16[8,72,2304]{2,1,0:T(8,128)(2,1)} async-done(((bf16[8,72,2304]{2,1,0:T(8,128)(2,1)}), bf16[8,72,2304]{2,1,0:T(8,128)(2,1)}, u32[]{:S(2)}, u32[]{:S(2)}) %all-to-all-start.3) | async-done | bytes 2654240 | tf_op jit(solution)/shard_map/all_to_all | solution.py:230
  294.6 5.9 %convolution_convert_fusion.1 = bf16[256,2304]{1,0:T(8,128)(2,1)} fusion(f32[256,576]{0,1:T(8,128)S(1)} %select_reduce_fusion, bf16[576,2304]{1,0:T(8,128)(2,1)} %bitcast.65), kind=kOutput, calls=%fused_computation.12 | convolution fusion | flops 4077453312 | bytes 4423680 | tf_op jit(solution)/shard_map/dot_general | solution.py:236
  302.5 3.0 reshape.581
  305.5 6.7 %copy.94 = bf16[6,128,2,576]{1,3,2,0:T(8,128)(2,1)} copy(bf16[6,128,2,576]{3,2,1,0:T(2,128)(2,1)} %reshape.581) | data formatting | bytes 3538944
  312.2 41.7 %all-reduce.5.cloned.1.call-done = bf16[256,2304]{1,0:T(8,128)(2,1)} async-done(((bf16[256,2304]{1,0:T(8,128)(2,1)}), bf16[256,2304]{1,0:T(8,128)(2,1)}) %all-reduce.5.cloned.1.call-update) | async-done | bytes 1179664 | tf_op jit(solution)/shard_map/psum | solution.py:237
  353.8 3.7 %add_convert_fusion = bf16[256,2304]{1,0:T(8,128)(2,1)} fusion(bf16[256,2304]{1,0:T(8,128)(2,1)} %all-reduce.5.cloned.1.call-done, f32[256,2304]{1,0:T(8,128)} %all-reduce.3.cloned.1.call-done, bf16[256,2304]{1,0:T(8,128)(2,1)} %param.18), kind=kLoop, calls=%fused_computation.22 | loop fusion | flops 2949120 | bytes 5898240 | tf_op jit(solution)/shard_map/convert_element_type | solution.py:238
  (118 shorter events, 24.6 us)
Async XLA Ops:
  7.2 79.4 %copy-start = (bf16[576,2304]{1,0:T(8,128)(2,1)S(1)}, bf16[576,2304]{1,0:T(8,128)(2,1)}, u32[]{:S(2)}) copy-start(bf16[576,2304]{1,0:T(8,128)(2,1)} %param.27) | copy-start | bytes 7962628
  7.2 44.8 %copy-start.14 = (bf16[2,16,3,576]{3,1,2,0:T(8,128)(2,1)S(1)}, bf16[2,16,3,576]{3,1,2,0:T(8,128)(2,1)}, u32[]{:S(2)}) copy-start(bf16[2,16,3,576]{3,1,2,0:T(8,128)(2,1)} %param.33) | copy-start | bytes 331780
  7.2 57.0 %copy-start.18 = (f32[2304]{0:T(1024)S(1)}, f32[2304]{0:T(1024)}, u32[]{:S(2)}) copy-start(f32[2304]{0:T(1024)} %param.24) | copy-start | bytes 27652
  7.2 63.8 %all-gather.3.cloned.1.call-start = ((), (), s32[]{:S(2)}) async-start(), calls=%async_computation.4 | async-start | bytes 5308416 | tf_op jit(solution)/shard_map/all_gather | solution.py:74
  7.9 76.1 %all-gather.5.cloned.1.call-start = ((), (), s32[]{:S(2)}) async-start(), calls=%async_computation.5 | async-start | bytes 1327104 | tf_op jit(solution)/shard_map/all_gather | solution.py:77
  8.7 176.3 %all-reduce.3.cloned.1.call-start = ((), (), s32[]{:S(2)}) async-start(), calls=%async_computation.6 | async-start | bytes 4718592 | tf_op jit(solution)/shard_map/psum | solution.py:154
  10.4 53.8 %copy-start.5 = (bf16[256,2304]{1,0:T(8,128)(2,1)S(1)}, bf16[256,2304]{1,0:T(8,128)(2,1)}, u32[]{:S(2)}) copy-start(bf16[256,2304]{1,0:T(8,128)(2,1)} %param.18) | copy-start | bytes 3538948
  71.0 1.5 copy-start.6
  71.0 2.5 slice-start
  73.6 1.3 copy-start.9
  73.6 1.8 copy-start.10
  75.9 1.2 copy-start.8
  78.1 3.4 copy-start.12
  89.2 0.7 copy-start.16
  93.1 97.8 %all-to-all-start.1 = ((bf16[8,1,72]{2,1,0:T(2,128)(2,1)}), bf16[8,1,72]{2,1,0:T(2,128)(2,1)S(1)}, u32[]{:S(2)}, u32[]{:S(2)}) async-start(bf16[8,1,72]{2,1,0:T(2,128)(2,1)} %all_to_all.20), calls=%async_computation.1 | async-start | bytes 8192 | tf_op jit(solution)/shard_map/all_to_all | solution.py:203
  96.6 90.9 %copy-start.17 = (f32[2304]{0:T(1024)S(1)}, f32[2304]{0:T(1024)}, u32[]{:S(2)}) copy-start(f32[2304]{0:T(1024)} %param.25) | copy-start | bytes 27652
  185.0 2.7 copy-start.2
  185.0 3.0 copy-start.7
  188.0 1.5 slice-start.1
  188.4 1.0 copy-start.3
  190.9 8.5 %all-to-all-start.2 = ((bf16[8,72,16]{1,2,0:T(8,128)(2,1)}), bf16[8,72,16]{1,2,0:T(8,128)(2,1)S(1)}, u32[]{:S(2)}, u32[]{:S(2)}) async-start(bf16[8,72,16]{1,2,0:T(8,128)(2,1)} %copy.92), calls=%async_computation.2 | async-start | bytes 65536 | tf_op jit(solution)/shard_map/all_to_all | solution.py:200
  199.4 36.2 %all-to-all-start = ((bf16[8,72,2304]{2,1,0:T(8,128)(2,1)}), bf16[8,72,2304]{2,1,0:T(8,128)(2,1)S(1)}, u32[]{:S(2)}, u32[]{:S(2)}) async-start(bf16[8,72,2304]{2,1,0:T(8,128)(2,1)} %bitcast.55), calls=%async_computation | async-start | bytes 5308416 | tf_op jit(solution)/shard_map/all_to_all | solution.py:197
  235.6 11.4 %copy-start.11 = (bf16[1,256,2,1440]{1,3,2,0:T(8,128)(2,1)S(1)}, bf16[1,256,2,1440]{1,3,2,0:T(8,128)(2,1)}, u32[]{:S(2)}) copy-start(bf16[1,256,2,1440]{1,3,2,0:T(8,128)(2,1)} %param.31) | copy-start | bytes 4423684
  257.5 5.1 %copy-start.4 = (bf16[256,2304]{1,0:T(8,128)(2,1)S(1)}, bf16[256,2304]{1,0:T(8,128)(2,1)}, u32[]{:S(2)}) copy-start(bf16[256,2304]{1,0:T(8,128)(2,1)} %copy-done.3) | copy-start | bytes 3538948
  257.5 5.1 %copy-start.15 = (bf16[2304,8]{0,1:T(8,128)(2,1)S(1)}, bf16[2304,8]{0,1:T(8,128)(2,1)}, u32[]{:S(2)}) copy-start(bf16[2304,8]{0,1:T(8,128)(2,1)} %param.28) | copy-start | bytes 110596
  257.5 37.1 %all-to-all-start.3 = ((bf16[8,72,2304]{2,1,0:T(8,128)(2,1)}), bf16[8,72,2304]{2,1,0:T(8,128)(2,1)}, u32[]{:S(2)}, u32[]{:S(2)}) async-start(bf16[8,72,2304]{2,1,0:T(8,128)(2,1)} %bitcast.152), calls=%async_computation.3 | async-start | bytes 5308416 | tf_op jit(solution)/shard_map/all_to_all | solution.py:230
  262.0 91.8 %all-reduce.5.cloned.1.call-start = ((), (), s32[]{:S(2)}) async-start(), calls=%async_computation.7 | async-start | bytes 2359296 | tf_op jit(solution)/shard_map/psum | solution.py:237
  294.6 7.0 %copy-start.13 = (bf16[256,9,32]{0,2,1:T(8,128)(2,1)S(1)}, bf16[256,9,32]{0,2,1:T(8,128)(2,1)}, u32[]{:S(2)}) copy-start(bf16[256,9,32]{0,2,1:T(8,128)(2,1)} %copy-done.12) | copy-start | bytes 442372
  305.5 52.0 %copy-start.1 = (bf16[576,2304]{1,0:T(8,128)(2,1)S(1)}, bf16[576,2304]{1,0:T(8,128)(2,1)}, u32[]{:S(2)}) copy-start(bf16[576,2304]{1,0:T(8,128)(2,1)} %param.27) | copy-start | bytes 7962628
Sparse Core Ops, SparseCore 0:
  9.9 42.8 all-gather.2
  54.7 24.0 all-gather.4
  89.3 95.5 all-reduce.2
  300.6 53.1 all-reduce.4
where the time goes:
time: 365 us; the launch traced here: 364 us
  waiting for transfers between devices  192 us (53%)
  matrix products  52.9 us (14%)
  other arithmetic  35.5 us (10%)
  local copies, waits for them, and re-layouts  29.5 us (8%)
  blocking collectives  24 us (7%)
  starting transfers between devices  15.6 us (4%)
  between operations  14.2 us (4%)
    psum x1, waiting for transfers between devices, per_device(): mixed_out = lax.psum(head_term, 'tp')  88.4 us
    psum x1, waiting for transfers between devices, per_device(): moe_sum = lax.psum(moe_part.astype(jnp.bfloat16), 'tp').astype(jnp.float32)  41.7 us
    all_to_all x1, waiting for transfers between devices, per_device(): lax.all_to_all(spread_copies(send_rows), 'req', split_axis=0, concat_axis...  32.1 us
    all_to_all x1, waiting for transfers between devices, per_device(): lax.all_to_all(partial_term.reshape(n_req, count, D), 'req', split_axis=0...  27.5 us
    gather x3, other arithmetic, per_device(): token_slot = slot_of[adapter]  12.5 us
    unnamed x40, local copies, waits for them, and re-layouts  12.2 us
    all_gather x1, blocking collectives, per_device(): lax.all_gather(pool_aout, 'req', axis=0, tiled=True)  12 us
    all_gather x1, blocking collectives, per_device(): lax.all_gather(slot_query_key_value_up, 'req', axis=0, tiled=True)  12 us
  transfers between devices with their start and end apart: 8, of which 5 were waited for; matrix products, arithmetic and copies ran while one was open for 20% of the time, Pallas kernels for 0%

commit v1 on v0

--- a/solution.py
+++ b/solution.py
@@ -14,6 +14,18 @@
 epsilon = 1e-05
 adapter_scale = 2.0
 rope_base = 10000.0
+
+
+def collect(x, axis, dim):
+    ways, here = (lax.axis_size(axis), lax.axis_index(axis))
+    grown, reach = (x, 1)
+    while reach < ways:
+        theirs = lax.ppermute(grown, axis, [(d, d ^ reach) for d in range(ways)])
+        mine_first = jnp.concatenate([grown, theirs], axis=dim)
+        theirs_first = jnp.concatenate([theirs, grown], axis=dim)
+        grown = jnp.where(here & reach == 0, mine_first, theirs_first)
+        reach = 2 * reach
+    return grown
 
 
 def rms_norm(values, scales):
@@ -73,7 +85,7 @@
     pool_down, slot_up_factors, pool_head, pool_outup = (
         lax.all_gather(pool_a, "req", axis=0, tiled=True),
         lax.all_gather(slot_query_key_value_up, "req", axis=0, tiled=True),
-        lax.all_gather(pool_aout, "req", axis=0, tiled=True),
+        collect(pool_aout, "req", 0),
         lax.all_gather(pool_bout, "req", axis=0, tiled=True),
     )
     slot_count = pool_down.shape[0]

time: 365 us -> 363 us (level)
  blocking collectives: 24 us -> 12.8 us
  starting transfers between devices: 15.6 us -> 20.6 us
    all_gather x1 -> x0, blocking collectives: 12 us -> none  [per_device(): lax.all_gather(pool_aout, 'req', axis=0, tiled=True)]
    ppermute x0 -> x3, starting transfers between devices: none -> 5 us  [collect(): theirs = lax.ppermute(grown, axis, [(d, d ^ reach) for d in range(ways)])]
  transfers between devices with their start and end apart: 8 -> 11, of which waited for: 5 -> 6; matrix products, arithmetic and copies ran while one was open for 20% -> 21% of each run, Pallas kernels for 0% -> 0%
where the time goes in v1:
time: 363 us; the launch traced here: 362 us
  waiting for transfers between devices  195 us (54%)
  matrix products  53.9 us (15%)
  other arithmetic  35.5 us (10%)
  local copies, waits for them, and re-layouts  29.4 us (8%)
  starting transfers between devices  20.6 us (6%)
  between operations  14.3 us (4%)
  blocking collectives  12.8 us (4%)
    psum x1, waiting for transfers between devices, per_device(): mixed_out = lax.psum(head_term, 'tp')  89.2 us
    psum x1, waiting for transfers between devices, per_device(): moe_sum = lax.psum(moe_part.astype(jnp.bfloat16), 'tp').astype(jnp.float32)  41.7 us
    all_to_all x1, waiting for transfers between devices, per_device(): lax.all_to_all(spread_copies(send_rows), 'req', split_axis=0, concat_axis...  32.1 us
    all_to_all x1, waiting for transfers between devices, per_device(): lax.all_to_all(partial_term.reshape(n_req, count, D), 'req', split_axis=0...  27.5 us
    all_gather x1, blocking collectives, per_device(): lax.all_gather(slot_query_key_value_up, 'req', axis=0, tiled=True)  12.8 us
    gather x3, other arithmetic, per_device(): token_slot = slot_of[adapter]  12.5 us
    unnamed x40, local copies, waits for them, and re-layouts  12 us
    dot_general x1, matrix products, per_device(): jnp.dot(flat_rows, w_gate_up[0].reshape(D, 2 * unit_count), preferred_ele...  11.4 us
  transfers between devices with their start and end apart: 11, of which 6 were waited for; matrix products, arithmetic and copies ran while one was open for 21% of the time, Pallas kernels for 0%

profile of v1, /device:TPU:0, one launch (start us, length us, event | category | flops | bytes accessed | tf_op | source)
XLA Modules:
  0.0 361.6 jit_solution(46273070635351321)
XLA Ops:
  11.1 1.6 fusion.10
  14.2 1.6 fusion.66
  15.8 1.9 fusion.62
  17.7 6.8 %compare_select_fusion.9 = (s32[256,1]{0,1:T(1,128)S(1)}, s32[256,1]{0,1:T(1,128)S(1)}, s32[256,1]{0,1:T(1,128)S(1)}) fusion(s32[]{:T(128)} %bitcast.20, s32[]{:T(128)} %bitcast.21, s32[]{:T(128)} %bitcast.22, s32[]{:T(128)} %bitcast.23, s32[]{:T(128)} %bitcast.24, s32[]{:T(128)} %bitcast.26, s32[]{:T(128)} %bitcast.25, s32[]{:T(128)} %bitcast.10, ...), kind=kLoop, calls=%fused_computation.108 | loop fusion | flops 6144 | bytes 4140 | tf_op jit(solution)/shard_map/gather | solution.py:84
  25.3 8.8 %fusion.49 = (s32[256,1]{0,1:T(1,128)S(1)}, s32[256,1]{0,1:T(1,128)S(1)}) fusion(s32[]{:T(128)} %bitcast.71, s32[]{:T(128)} %bitcast.72, s32[]{:T(128)} %bitcast.73, s32[]{:T(128)} %bitcast.67, s32[]{:T(128)} %bitcast.74, s32[]{:T(128)} %bitcast.68, s32[]{:T(128)} %bitcast.76, s32[]{:T(128)} %bitcast.75, s32[]{:T(128)} %bitcast.70, s32[]{:T(128)} %bitcast.69, ...), kind=kLoop, calls=%fused_computation.135 | loop fusion | flops 11008 | bytes 3128 | tf_op jit(solution)/shard_map/mul | solution.py:124
  34.4 7.9 %fusion.1 = f32[256,3,576]{0,2,1:T(8,128)} fusion(bf16[2304,3,576]{0,2,1:T(8,128)(2,1)} %param.26, bf16[256,2304]{1,0:T(8,128)(2,1)} %param.18, f32[2304]{0:T(1024)} %param.24, f32[256]{0:T(256)S(1)} %add_rsqrt_fusion.1), kind=kOutput, calls=%fused_computation.2 | convolution fusion | flops 2040791040 | bytes 10921984 | tf_op jit(solution)/shard_map/dot_general | solution.py:111
  42.3 5.6 %select_select_fusion.2 = s32[256]{0:T(256)S(1)} fusion(pred[256]{0:T(512)(128)(4,1)S(1)} %get-tuple-element.22, pred[256]{0:T(512)(128)(4,1)S(1)} %get-tuple-element.21, pred[256]{0:T(512)(128)(4,1)S(1)} %get-tuple-element.20, pred[256]{0:T(512)(128)(4,1)S(1)} %get-tuple-element.19, pred[256]{0:T(512)(128)(4,1)S(1)} %get-tuple-element.18, ...), kind=kLoop, calls=%fused_computation.140 | loop fusion | flops 2304 | bytes 4388 | tf_op jit(solution)/shard_map/gather | solution.py:84
  48.0 2.4 collective-permute-start.1
  50.4 2.5 collective-permute-done.1
  52.9 2.1 collective-permute-start.2
  55.0 12.8 %all_gather.10 = bf16[16,16,3,576]{3,1,2,0:T(8,128)(2,1)} all-gather(bf16[2,16,3,576]{3,1,2,0:T(8,128)(2,1)S(1)} %copy-done.13), channel_id=1, replica_groups=mesh['req'=8,'tp'=4] {'req'}, dimensions={0}, use_global_device_ids=true | all-gather | bytes 995328 | tf_op jit(solution)/shard_map/all_gather | solution.py:87
  74.8 3.4 fusion.67
  78.2 2.2 convolution_convert_fusion.3
  80.8 2.5 fusion.8
  83.3 2.6 convolution_add_fusion
  89.9 3.4 all-to-all-start.1
  93.3 89.2 %all-reduce.3.cloned.1.call-done = f32[256,2304]{1,0:T(8,128)} async-done(((f32[256,2304]{1,0:T(8,128)}), f32[256,2304]{1,0:T(8,128)}) %all-reduce.3.cloned.1.call-update) | async-done | bytes 2359312 | tf_op jit(solution)/shard_map/psum | solution.py:166
  182.5 2.5 multiply_reduce_fusion
  188.5 3.7 %all-to-all-start.2 = ((bf16[8,72,16]{1,2,0:T(8,128)(2,1)}), bf16[8,72,16]{1,2,0:T(8,128)(2,1)S(1)}, u32[]{:S(2)}, u32[]{:S(2)}) async-start(bf16[8,72,16]{1,2,0:T(8,128)(2,1)} %copy.92), calls=%async_computation.2 | async-start | bytes 65536 | tf_op jit(solution)/shard_map/all_to_all | solution.py:212
  192.1 3.7 %convolution_convert_fusion = bf16[576,2304]{1,0:T(8,128)(2,1)} fusion(pred[256,576]{0,1:T(8,128)(4,1)S(1)} %fusion.17, bf16[256,2304]{1,0:T(8,128)(2,1)} %copy-done.3), kind=kOutput, calls=%fused_computation.8 | convolution fusion | flops 680804352 | bytes 3981312 | tf_op jit(solution)/shard_map/ts,td->sd/dot_general | solution.py:206
  197.0 3.6 %all-to-all-start = ((bf16[8,72,2304]{2,1,0:T(8,128)(2,1)}), bf16[8,72,2304]{2,1,0:T(8,128)(2,1)S(1)}, u32[]{:S(2)}, u32[]{:S(2)}) async-start(bf16[8,72,2304]{2,1,0:T(8,128)(2,1)} %bitcast.55), calls=%async_computation | async-start | bytes 5308416 | tf_op jit(solution)/shard_map/all_to_all | solution.py:209
  201.0 32.1 %all-to-all-done = bf16[8,72,2304]{2,1,0:T(8,128)(2,1)S(1)} async-done(((bf16[8,72,2304]{2,1,0:T(8,128)(2,1)}), bf16[8,72,2304]{2,1,0:T(8,128)(2,1)S(1)}, u32[]{:S(2)}, u32[]{:S(2)}) %all-to-all-start) | async-done | bytes 2654240 | tf_op jit(solution)/shard_map/all_to_all | solution.py:209
  233.1 11.4 %fusion.72 = f32[576,2880]{1,0:T(8,128)S(1)} fusion(bf16[576,2304]{1,0:T(8,128)(2,1)S(1)} %bitcast.153, bf16[2304,2880]{0,1:T(8,128)(2,1)} %bitcast.173), kind=kOutput, calls=%fused_computation.168 | convolution fusion | flops 7644119040 | bytes 22560768 | tf_op jit(solution)/shard_map/dot_general | solution.py:228
  245.8 9.2 %fusion.5 = bf16[576,2304]{1,0:T(8,128)(2,1)} fusion(bf16[1,1440,2304]{2,1,0:T(8,128)(2,1)} %param.30, f32[576,2880]{1,0:T(8,128)S(1)} %multiply_add_fusion), kind=kOutput, calls=%fused_computation.7 | convolution fusion | flops 3828363264 | bytes 16367616 | tf_op jit(solution)/shard_map/dot_general | solution.py:239
  255.0 4.5 %all-to-all-start.3 = ((bf16[8,72,2304]{2,1,0:T(8,128)(2,1)}), bf16[8,72,2304]{2,1,0:T(8,128)(2,1)}, u32[]{:S(2)}, u32[]{:S(2)}) async-start(bf16[8,72,2304]{2,1,0:T(8,128)(2,1)} %bitcast.152), calls=%async_computation.3 | async-start | bytes 5308416 | tf_op jit(solution)/shard_map/all_to_all | solution.py:242
  260.5 3.6 gather_fusion
  264.6 27.5 %all-to-all-done.3 = bf16[8,72,2304]{2,1,0:T(8,128)(2,1)} async-done(((bf16[8,72,2304]{2,1,0:T(8,128)(2,1)}), bf16[8,72,2304]{2,1,0:T(8,128)(2,1)}, u32[]{:S(2)}, u32[]{:S(2)}) %all-to-all-start.3) | async-done | bytes 2654240 | tf_op jit(solution)/shard_map/all_to_all | solution.py:242
  292.2 5.9 %convolution_convert_fusion.1 = bf16[256,2304]{1,0:T(8,128)(2,1)} fusion(f32[256,576]{0,1:T(8,128)S(1)} %select_reduce_fusion, bf16[576,2304]{1,0:T(8,128)(2,1)} %bitcast.65), kind=kOutput, calls=%fused_computation.12 | convolution fusion | flops 4077453312 | bytes 4423680 | tf_op jit(solution)/shard_map/dot_general | solution.py:248
  300.0 3.0 reshape.581
  303.0 6.7 %copy.94 = bf16[6,128,2,576]{1,3,2,0:T(8,128)(2,1)} copy(bf16[6,128,2,576]{3,2,1,0:T(2,128)(2,1)} %reshape.581) | data formatting | bytes 3538944
  309.7 41.7 %all-reduce.5.cloned.1.call-done = bf16[256,2304]{1,0:T(8,128)(2,1)} async-done(((bf16[256,2304]{1,0:T(8,128)(2,1)}), bf16[256,2304]{1,0:T(8,128)(2,1)}) %all-reduce.5.cloned.1.call-update) | async-done | bytes 1179664 | tf_op jit(solution)/shard_map/psum | solution.py:249
  351.3 3.7 %add_convert_fusion = bf16[256,2304]{1,0:T(8,128)(2,1)} fusion(bf16[256,2304]{1,0:T(8,128)(2,1)} %all-reduce.5.cloned.1.call-done, f32[256,2304]{1,0:T(8,128)} %all-reduce.3.cloned.1.call-done, bf16[256,2304]{1,0:T(8,128)(2,1)} %param.18), kind=kLoop, calls=%fused_computation.22 | loop fusion | flops 2949120 | bytes 5898240 | tf_op jit(solution)/shard_map/convert_element_type | solution.py:250
  (126 shorter events, 27.5 us)
Async XLA Ops:
  7.2 76.1 %copy-start = (bf16[576,2304]{1,0:T(8,128)(2,1)S(1)}, bf16[576,2304]{1,0:T(8,128)(2,1)}, u32[]{:S(2)}) copy-start(bf16[576,2304]{1,0:T(8,128)(2,1)} %param.27) | copy-start | bytes 7962628
  7.2 60.8 %all-gather.3.cloned.1.call-start = ((), (), s32[]{:S(2)}) async-start(), calls=%async_computation.4 | async-start | bytes 5308416 | tf_op jit(solution)/shard_map/all_gather | solution.py:86
  7.9 72.9 %all-gather.5.cloned.1.call-start = ((), (), s32[]{:S(2)}) async-start(), calls=%async_computation.5 | async-start | bytes 1327104 | tf_op jit(solution)/shard_map/all_gather | solution.py:89
  8.0 40.0 %collective-permute-start = (bf16[2,576,16]{1,2,0:T(8,128)(2,1)}, bf16[2,576,16]{1,2,0:T(8,128)(2,1)S(1)}, u32[]{:S(2)}, u32[]{:S(2)}) collective-permute-start(bf16[2,576,16]{1,2,0:T(8,128)(2,1)} %param.34), channel_id=1, source_target_pairs={{0,4},{4,0},{8,12},{12,8},{16,20},{20,16},{24,28},{28,24},{1,5},{5... | collective-permute-start | bytes 110600 | tf_op jit(solution)/shard_map/ppermute | solution.py:23
  8.7 173.8 %all-reduce.3.cloned.1.call-start = ((), (), s32[]{:S(2)}) async-start(), calls=%async_computation.6 | async-start | bytes 4718592 | tf_op jit(solution)/shard_map/psum | solution.py:166
  34.4 13.5 %copy-start.14 = (bf16[2,576,16]{1,2,0:T(8,128)(2,1)S(1)}, bf16[2,576,16]{1,2,0:T(8,128)(2,1)}, u32[]{:S(2)}) copy-start(bf16[2,576,16]{1,2,0:T(8,128)(2,1)} %param.34) | copy-start | bytes 110596
  34.4 20.6 %copy-start.13 = (bf16[2,16,3,576]{3,1,2,0:T(8,128)(2,1)S(1)}, bf16[2,16,3,576]{3,1,2,0:T(8,128)(2,1)}, u32[]{:S(2)}) copy-start(bf16[2,16,3,576]{3,1,2,0:T(8,128)(2,1)} %param.33) | copy-start | bytes 331780
  48.0 4.9 %collective-permute-start.1 = (bf16[4,576,16]{1,2,0:T(8,128)(2,1)S(1)}, bf16[4,576,16]{1,2,0:T(8,128)(2,1)S(1)}, u32[]{:S(2)}, u32[]{:S(2)}) collective-permute-start(bf16[4,576,16]{1,2,0:T(8,128)(2,1)S(1)} %maximum_select_fusion.2), channel_id=1, source_target_pairs={{0,8},{4,12},{8,0},{12,4},{16,24},{20,28},{24,16},{28,20},{1,9},{5... | collective-permute-start | bytes 221192 | tf_op jit(solution)/shard_map/ppermute | solution.py:23
  52.9 14.9 %collective-permute-start.2 = (bf16[8,576,16]{1,2,0:T(8,128)(2,1)S(1)}, bf16[8,576,16]{1,2,0:T(8,128)(2,1)S(1)}, u32[]{:S(2)}, u32[]{:S(2)}) collective-permute-start(bf16[8,576,16]{1,2,0:T(8,128)(2,1)S(1)} %maximum_select_fusion.1), channel_id=1, source_target_pairs={{0,16},{4,20},{8,24},{12,28},{16,0},{20,4},{24,8},{28,12},{1,17},{... | collective-permute-start | bytes 442376 | tf_op jit(solution)/shard_map/ppermute | solution.py:23
  67.9 0.7 copy-start.18
  67.9 1.3 copy-start.5
  68.0 2.3 slice-start
  70.3 1.3 copy-start.8
  70.3 1.8 copy-start.9
  72.6 1.2 copy-start.7
  74.8 3.4 copy-start.11
  85.9 0.7 copy-start.16
  89.9 98.6 %all-to-all-start.1 = ((bf16[8,1,72]{2,1,0:T(2,128)(2,1)}), bf16[8,1,72]{2,1,0:T(2,128)(2,1)S(1)}, u32[]{:S(2)}, u32[]{:S(2)}) async-start(bf16[8,1,72]{2,1,0:T(2,128)(2,1)} %all_to_all.20), calls=%async_computation.1 | async-start | bytes 8192 | tf_op jit(solution)/shard_map/all_to_all | solution.py:215
  93.3 91.7 %copy-start.17 = (f32[2304]{0:T(1024)S(1)}, f32[2304]{0:T(1024)}, u32[]{:S(2)}) copy-start(f32[2304]{0:T(1024)} %param.25) | copy-start | bytes 27652
  182.5 2.7 copy-start.2
  182.5 3.0 copy-start.6
  185.5 1.5 slice-start.1
  186.0 1.0 copy-start.3
  188.5 8.5 %all-to-all-start.2 = ((bf16[8,72,16]{1,2,0:T(8,128)(2,1)}), bf16[8,72,16]{1,2,0:T(8,128)(2,1)S(1)}, u32[]{:S(2)}, u32[]{:S(2)}) async-start(bf16[8,72,16]{1,2,0:T(8,128)(2,1)} %copy.92), calls=%async_computation.2 | async-start | bytes 65536 | tf_op jit(solution)/shard_map/all_to_all | solution.py:212
  197.0 36.2 %all-to-all-start = ((bf16[8,72,2304]{2,1,0:T(8,128)(2,1)}), bf16[8,72,2304]{2,1,0:T(8,128)(2,1)S(1)}, u32[]{:S(2)}, u32[]{:S(2)}) async-start(bf16[8,72,2304]{2,1,0:T(8,128)(2,1)} %bitcast.55), calls=%async_computation | async-start | bytes 5308416 | tf_op jit(solution)/shard_map/all_to_all | solution.py:209
  233.1 11.4 %copy-start.10 = (bf16[1,256,2,1440]{1,3,2,0:T(8,128)(2,1)S(1)}, bf16[1,256,2,1440]{1,3,2,0:T(8,128)(2,1)}, u32[]{:S(2)}) copy-start(bf16[1,256,2,1440]{1,3,2,0:T(8,128)(2,1)} %param.31) | copy-start | bytes 4423684
  255.0 5.1 %copy-start.4 = (bf16[256,2304]{1,0:T(8,128)(2,1)S(1)}, bf16[256,2304]{1,0:T(8,128)(2,1)}, u32[]{:S(2)}) copy-start(bf16[256,2304]{1,0:T(8,128)(2,1)} %copy-done.3) | copy-start | bytes 3538948
  255.0 5.1 %copy-start.15 = (bf16[2304,8]{0,1:T(8,128)(2,1)S(1)}, bf16[2304,8]{0,1:T(8,128)(2,1)}, u32[]{:S(2)}) copy-start(bf16[2304,8]{0,1:T(8,128)(2,1)} %param.28) | copy-start | bytes 110596
  255.0 37.1 %all-to-all-start.3 = ((bf16[8,72,2304]{2,1,0:T(8,128)(2,1)}), bf16[8,72,2304]{2,1,0:T(8,128)(2,1)}, u32[]{:S(2)}, u32[]{:S(2)}) async-start(bf16[8,72,2304]{2,1,0:T(8,128)(2,1)} %bitcast.152), calls=%async_computation.3 | async-start | bytes 5308416 | tf_op jit(solution)/shard_map/all_to_all | solution.py:242
  259.5 91.8 %all-reduce.5.cloned.1.call-start = ((), (), s32[]{:S(2)}) async-start(), calls=%async_computation.7 | async-start | bytes 2359296 | tf_op jit(solution)/shard_map/psum | solution.py:249
  292.2 7.0 %copy-start.12 = (bf16[256,9,32]{0,2,1:T(8,128)(2,1)S(1)}, bf16[256,9,32]{0,2,1:T(8,128)(2,1)}, u32[]{:S(2)}) copy-start(bf16[256,9,32]{0,2,1:T(8,128)(2,1)} %copy-done.11) | copy-start | bytes 442372
  303.0 52.0 %copy-start.1 = (bf16[576,2304]{1,0:T(8,128)(2,1)S(1)}, bf16[576,2304]{1,0:T(8,128)(2,1)}, u32[]{:S(2)}) copy-start(bf16[576,2304]{1,0:T(8,128)(2,1)} %param.27) | copy-start | bytes 7962628
Sparse Core Ops, SparseCore 0:
  9.9 41.6 all-gather.2
  53.4 25.3 all-gather.4
  86.1 96.3 all-reduce.2
  298.2 53.1 all-reduce.4
